TPU v7x, 32 devices: a whole 2x2x4 slice. The times are simulated.
32 devices in a mesh: groups: 2 (over x), dp: 16 (over z, y, core).
Axes of the slice: x: 2, y: 2, z: 4, core: 2. Of those that a mesh axis runs over, the one named last changes fastest.
Arguments:
- queries: bfloat16 [16384, 1024], P(('groups', 'dp')), parts along dimension 0, may hold values from -5.5 to 5.5
- kv_cache: bfloat16 [16384, 256], P(('groups', 'dp')), parts along dimension 0, may hold values from -5.5 to 5.5
- grad_out: bfloat16 [16384, 1024], P(('groups', 'dp')), parts along dimension 0, may hold values from -48 to 48
- pair_lengths: int32 [20], P('groups'), parts along dimension 0, may hold values from 1 to 12, 32 in all
Outputs:
- grad_queries: bfloat16 [16384, 1024], P(('groups', 'dp')), parts along dimension 0
- grad_kv: float32 [16384, 256], P(('groups', 'dp')), parts along dimension 0
There are 2 independent parts, one for each index of `groups`. A program takes and returns all parts, laid end to end along the dimension named above; each array names one. Nothing has to cross between parts.
Inputs may be any that keep to these rules, and one draw needn't show every extreme that they name: `pair_lengths`: the 10 lengths sum to 32; the longest is exactly 12.
All inputs are finite; a program needn't handle non-finite values.
Results may differ from a plain program's by a relative error of at most 0.0078.
Values may be sent and summed in bfloat16 or wider, within the bound.
No kernel may reach another device: no remote copies, remote signals or barrier semaphores. Data moves between devices by JAX's collectives and lax.ppermute only.
A program may use at most 192 MiB of HBM per device.

v0:
```python
import jax
import jax.numpy as jnp
from jax import lax
from jax.sharding import PartitionSpec as P

HD = 128
QH = 8
HG = 4
TILE = 256
MOST = 12


def passed_along(value, axis, steps):
    count = lax.axis_size(axis)
    initial, last = (max(0, -steps), min(count, count - steps))
    return lax.ppermute(value, axis, [(source, source + steps) for source in range(initial, last)])


def pair_span(pair_lengths, tile_index):
    pair_ends = jnp.cumsum(pair_lengths)
    pair_starts = pair_ends - pair_lengths
    inside = (tile_index >= pair_starts) & (tile_index < pair_ends)
    first = jnp.sum(jnp.where(inside, pair_starts, 0))
    count = jnp.sum(jnp.where(inside, pair_lengths, 0))
    return (first, count)


def unit_grads(unit_queries, unit_grads_out, windows, counts):
    softmax_scale = HD ** (-0.5)
    unit_count = unit_queries.shape[0]
    width = unit_queries.shape[2]
    heads = width // HD
    window_rows = windows.shape[1]
    blocks = window_rows // TILE

    def one_unit(unit_index, carry):
        grad_units, grad_windows = carry
        query_block = lax.dynamic_index_in_dim(unit_queries, unit_index, 0, keepdims=False).reshape(
            TILE, heads, HD
        )
        grad_block = lax.dynamic_index_in_dim(
            unit_grads_out, unit_index, 0, keepdims=False
        ).reshape(TILE, heads, HD)
        kv_rows = lax.dynamic_index_in_dim(windows, unit_index, 0, keepdims=False)
        count = counts[unit_index]

        def block_keys(block_index):
            kv_block = lax.dynamic_slice_in_dim(kv_rows, block_index * TILE, TILE, 0)
            return (kv_block[:, :HD], kv_block[:, HD:])

        def block_scores(block_index):
            key_block, value_block = block_keys(block_index)
            scores = (
                jnp.einsum(
                    "rgc,kc->rgk", query_block, key_block, preferred_element_type=jnp.float32
                )
                * softmax_scale
            )
            grad_probs = jnp.einsum(
                "rgc,kc->rgk", grad_block, value_block, preferred_element_type=jnp.float32
            )
            return (scores, grad_probs)

        def gather_stats(stats, scores, grad_probs):
            running_max, total, weighted = stats
            new_max = jnp.maximum(running_max, jnp.max(scores, axis=2))
            fading = jnp.exp(running_max - new_max)
            weights = jnp.exp(scores - new_max[:, :, None])
            total = total * fading + jnp.sum(weights, axis=2)
            weighted = weighted * fading + jnp.sum(weights * grad_probs, axis=2)
            return (new_max, total, weighted)

        start_stats = (
            jnp.full((TILE, heads), -jnp.inf, jnp.float32),
            jnp.zeros((TILE, heads), jnp.float32),
            jnp.zeros((TILE, heads), jnp.float32),
        )
        empty_store = jnp.zeros((blocks, TILE, heads, TILE), jnp.float32)

        def first_pass(block_index, state):
            stats, score_store, prob_store = state
            scores, grad_probs = block_scores(block_index)
            stats = gather_stats(stats, scores, grad_probs)
            score_store = lax.dynamic_update_index_in_dim(score_store, scores, block_index, 0)
            prob_store = lax.dynamic_update_index_in_dim(prob_store, grad_probs, block_index, 0)
            return (stats, score_store, prob_store)

        stats, score_store, prob_store = lax.fori_loop(
            0, count, first_pass, (start_stats, empty_store, empty_store)
        )

        def fetch(block_index):
            scores = lax.dynamic_index_in_dim(score_store, block_index, 0, keepdims=False)
            grad_probs = lax.dynamic_index_in_dim(prob_store, block_index, 0, keepdims=False)
            return (scores, grad_probs)

        running_max, total, weighted = stats
        log_total = running_max + jnp.log(total)
        row_delta = weighted / total

        def second_pass(block_index, state):
            grad_query, window_grad = state
            scores, grad_probs = fetch(block_index)
            key_block, value_block = block_keys(block_index)
            attention = jnp.exp(scores - log_total[:, :, None])
            attention_low = attention.astype(jnp.bfloat16)
            grad_scores = (attention * (grad_probs - row_delta[:, :, None])).astype(jnp.bfloat16)
            grad_query = grad_query + jnp.einsum(
                "rgk,kc->rgc", grad_scores, key_block, preferred_element_type=jnp.float32
            )
            grad_keys = (
                jnp.einsum(
                    "rgk,rgc->kc", grad_scores, query_block, preferred_element_type=jnp.float32
                )
                * softmax_scale
            )
            grad_values = jnp.einsum(
                "rgk,rgc->kc", attention_low, grad_block, preferred_element_type=jnp.float32
            )
            window_grad = lax.dynamic_update_slice_in_dim(
                window_grad,
                jnp.concatenate([grad_keys, grad_values], axis=1),
                block_index * TILE,
                0,
            )
            return (grad_query, window_grad)

        start_grads = (
            jnp.zeros((TILE, heads, HD), jnp.float32),
            jnp.zeros((window_rows, 2 * HD), jnp.float32),
        )
        grad_query, window_grad = lax.fori_loop(0, count, second_pass, start_grads)
        finished = (grad_query * softmax_scale).astype(jnp.bfloat16).reshape(TILE, width)
        grad_units = lax.dynamic_update_index_in_dim(grad_units, finished, unit_index, 0)
        grad_windows = lax.dynamic_update_index_in_dim(grad_windows, window_grad, unit_index, 0)
        return (grad_units, grad_windows)

    empty_units = jnp.zeros(unit_queries.shape, jnp.bfloat16)
    empty_windows = jnp.zeros(windows.shape, jnp.float32)
    return lax.fori_loop(0, unit_count, one_unit, (empty_units, empty_windows))


def body(queries, kv_cache, grad_out, pair_lengths):
    tok_dev = queries.shape[0]
    per_device = tok_dev // TILE
    head_groups = QH // HG
    width = HG * HD
    unit_count = per_device * head_groups
    my_index = lax.axis_index("dp")
    window_rows = MOST * TILE
    reach = (MOST - 1 + per_device - 1) // per_device
    pieces = []
    for distance in range(-reach, reach + 1):
        if distance == 0:
            pieces.append(kv_cache)
        else:
            pieces.append(passed_along(kv_cache, "dp", -distance))
    near_rows = jnp.concatenate(pieces, axis=0)
    base_row = (my_index - reach) * tok_dev
    unit_queries = (
        queries.reshape(per_device, TILE, head_groups, width)
        .transpose(0, 2, 1, 3)
        .reshape(unit_count, TILE, width)
    )
    unit_grads_out = (
        grad_out.reshape(per_device, TILE, head_groups, width)
        .transpose(0, 2, 1, 3)
        .reshape(unit_count, TILE, width)
    )
    unit_ids = jnp.arange(unit_count, dtype=jnp.int32)
    unit_tiles = my_index * per_device + unit_ids // head_groups
    span_of = jax.vmap(pair_span, in_axes=(None, 0))
    firsts, counts = span_of(pair_lengths, unit_tiles)
    begins = firsts * TILE - base_row

    def cut_window(begin):
        return lax.dynamic_slice_in_dim(near_rows, begin, window_rows, 0)

    own_windows = jax.vmap(cut_window)(begins)
    own_dq, own_win = unit_grads(unit_queries, unit_grads_out, own_windows, counts)

    def add_window(unit_index, grad_rows):
        begin = begins[unit_index]
        previous = lax.dynamic_slice_in_dim(grad_rows, begin, window_rows, 0)
        addition = lax.dynamic_index_in_dim(own_win, unit_index, 0, keepdims=False)
        return lax.dynamic_update_slice_in_dim(grad_rows, previous + addition, begin, 0)

    grad_rows = lax.fori_loop(
        0, unit_count, add_window, jnp.zeros((near_rows.shape[0], 2 * HD), jnp.float32)
    )
    grad_queries = (
        own_dq.reshape(per_device, head_groups, TILE, width)
        .transpose(0, 2, 1, 3)
        .reshape(tok_dev, QH * HD)
    )
    grad_kv = grad_rows[reach * tok_dev : (reach + 1) * tok_dev]
    for distance in range(-reach, reach + 1):
        if distance != 0:
            block_low = (distance + reach) * tok_dev
            grad_kv = grad_kv + passed_along(
                grad_rows[block_low : block_low + tok_dev].astype(jnp.bfloat16), "dp", distance
            ).astype(jnp.float32)
    return (grad_queries, grad_kv)


def solution(mesh):
    return jax.shard_map(
        body,
        mesh=mesh,
        in_specs=(
            P(("groups", "dp"), None),
            P(("groups", "dp"), None),
            P(("groups", "dp"), None),
            P("groups"),
        ),
        out_specs=(P(("groups", "dp"), None), P(("groups", "dp"), None)),
        check_vma=False,
    )
```

profile of v0, /device:TPU:26, one launch (start us, length us, event | category | flops | bytes accessed | tf_op | source)
XLA Modules:
  0.0 918.7 jit_solution(4036199862288176897)
XLA Ops:
  4.7 2.9 collective-permute-start.3
  26.7 2.7 collective-permute-start.6
  30.4 4.6 collective-permute-start.7
  36.0 4.2 collective-permute-start.8
  41.1 5.2 collective-permute-start.9
  53.3 5.6 collective-permute-done.10
  59.0 4.7 collective-permute-done.11
  63.7 11.2 %while.107 = (s32[]{:T(128)}, bf16[6656,256]{1,0:T(8,128)(2,1)S(1)}, s32[4,2]{0,1:T(2,128)S(1)}, bf16[4,3072,256]{2,1,0:T(8,128)(2,1)}, s32[]{:T(128)}) while((s32[]{:T(128)}, bf16[6656,256]{1,0:T(8,128)(2,1)S(1)}, s32[4,2]{0,1:T(2,128)S(1)}, bf16[4,3072,256]{2,1,0:T(8,128)(2,1)}, s32[]{:T(128)}) %tuple.145), condition=%wide.while_cond, body=%wide.while_body.sunk | while | flops 2 | bytes 3146841 | solution.py:177
  75.0 689.1 %while.105 = (s32[]{:T(128)}, bf16[4,256,512]{2,1,0:T(8,128)(2,1)}, f32[4,3072,256]{1,2,0:T(8,128)}, s32[4]{0:T(128)S(1)}, bf16[4,3072,256]{2,1,0:T(8,128)(2,1)}...) while((s32[]{:T(128)}, bf16[4,256,512]{2,1,0:T(8,128)(2,1)}, ...), condition=%wide.region_11.12_spmd, body=%wide.region_3.11_spmd.sunk | while | flops 339186688 | bytes 68470824 | solution.py:140
  76.4 2.7 dynamic-slice_bitcast_fusion.9
  79.7 6.0 broadcast.166
  85.7 6.1 broadcast.166.clone
  91.9 56.6 %while.108 = (s32[]{:T(128)}, f32[256,4]{0,1:T(4,128)S(1)}, f32[256,4]{0,1:T(4,128)S(1)}, f32[256,4]{0,1:T(4,128)S(1)}, f32[12,256,4,256]{1,3,2,0:T(8,128)}, /*i...) while((s32[]{:T(128)}, f32[256,4]{0,1:T(4,128)S(1)}, ...), condition=%wide.region_8.8_spmd, body=%wide.region_4.7_spmd.sunk | while | flops 135793664 | bytes 8065281 | solution.py:88
  151.5 89.7 %while.109 = (s32[]{:T(128)}, f32[256,4,128]{2,0,1:T(8,128)}, f32[3072,256]{0,1:T(8,128)}, s32[]{:T(128)}, f32[12,256,4,256]{1,3,2,0:T(8,128)}, /*index=5*/f32[2...) while((s32[]{:T(128)}, f32[256,4,128]{2,0,1:T(8,128)}, ...), condition=%wide.region_10.10_spmd, body=%wide.region_9.9_spmd.sunk | while | flops 203128832 | bytes 16593165 | solution.py:132
  241.2 3.9 bitcast_dynamic-update-slice_fusion.7
  248.6 2.7 dynamic-slice_bitcast_fusion.9
  251.9 6.0 broadcast.166
  258.0 6.1 broadcast.166.clone
  264.1 56.6 %while.108 = (s32[]{:T(128)}, f32[256,4]{0,1:T(4,128)S(1)}, f32[256,4]{0,1:T(4,128)S(1)}, f32[256,4]{0,1:T(4,128)S(1)}, f32[12,256,4,256]{1,3,2,0:T(8,128)}, /*i...) while((s32[]{:T(128)}, f32[256,4]{0,1:T(4,128)S(1)}, ...), condition=%wide.region_8.8_spmd, body=%wide.region_4.7_spmd.sunk | while | flops 135793664 | bytes 8065281 | solution.py:88
  323.7 89.7 %while.109 = (s32[]{:T(128)}, f32[256,4,128]{2,0,1:T(8,128)}, f32[3072,256]{0,1:T(8,128)}, s32[]{:T(128)}, f32[12,256,4,256]{1,3,2,0:T(8,128)}, /*index=5*/f32[2...) while((s32[]{:T(128)}, f32[256,4,128]{2,0,1:T(8,128)}, ...), condition=%wide.region_10.10_spmd, body=%wide.region_9.9_spmd.sunk | while | flops 203128832 | bytes 16593165 | solution.py:132
  413.4 3.9 bitcast_dynamic-update-slice_fusion.7
  424.2 6.0 broadcast.166
  430.3 6.1 broadcast.166.clone
  436.4 56.6 %while.108 = (s32[]{:T(128)}, f32[256,4]{0,1:T(4,128)S(1)}, f32[256,4]{0,1:T(4,128)S(1)}, f32[256,4]{0,1:T(4,128)S(1)}, f32[12,256,4,256]{1,3,2,0:T(8,128)}, /*i...) while((s32[]{:T(128)}, f32[256,4]{0,1:T(4,128)S(1)}, ...), condition=%wide.region_8.8_spmd, body=%wide.region_4.7_spmd.sunk | while | flops 135793664 | bytes 8065281 | solution.py:88
  496.0 89.7 %while.109 = (s32[]{:T(128)}, f32[256,4,128]{2,0,1:T(8,128)}, f32[3072,256]{0,1:T(8,128)}, s32[]{:T(128)}, f32[12,256,4,256]{1,3,2,0:T(8,128)}, /*index=5*/f32[2...) while((s32[]{:T(128)}, f32[256,4,128]{2,0,1:T(8,128)}, ...), condition=%wide.region_10.10_spmd, body=%wide.region_9.9_spmd.sunk | while | flops 203128832 | bytes 16593165 | solution.py:132
  585.7 4.0 bitcast_dynamic-update-slice_fusion.7
  596.6 6.0 broadcast.166
  602.6 6.1 broadcast.166.clone
  608.7 56.6 %while.108 = (s32[]{:T(128)}, f32[256,4]{0,1:T(4,128)S(1)}, f32[256,4]{0,1:T(4,128)S(1)}, f32[256,4]{0,1:T(4,128)S(1)}, f32[12,256,4,256]{1,3,2,0:T(8,128)}, /*i...) while((s32[]{:T(128)}, f32[256,4]{0,1:T(4,128)S(1)}, ...), condition=%wide.region_8.8_spmd, body=%wide.region_4.7_spmd.sunk | while | flops 135793664 | bytes 8065281 | solution.py:88
  668.4 89.7 %while.109 = (s32[]{:T(128)}, f32[256,4,128]{2,0,1:T(8,128)}, f32[3072,256]{0,1:T(8,128)}, s32[]{:T(128)}, f32[12,256,4,256]{1,3,2,0:T(8,128)}, /*index=5*/f32[2...) while((s32[]{:T(128)}, f32[256,4,128]{2,0,1:T(8,128)}, ...), condition=%wide.region_10.10_spmd, body=%wide.region_9.9_spmd.sunk | while | flops 203128832 | bytes 16593165 | solution.py:132
  758.0 3.9 bitcast_dynamic-update-slice_fusion.7
  764.1 3.2 broadcast_in_dim.54
  767.3 76.2 %while.106 = (s32[]{:T(128)}, f32[6656,256]{1,0:T(8,128)}, s32[4]{0:T(128)S(1)}, f32[4,3072,256]{1,2,0:T(8,128)}, s32[]{:T(128)}, /*index=5*/s32[]{:T(128)}, s32[]{:T(128)}) while((s32[]{:T(128)}, f32[6656,256]{1,0:T(8,128)}, s32[4]{0:T(128)S(1)}, f32[4,3072,256]{1,2,0:T(8,128)}, s32[]{:T(128)}, /*index=5*/s32[]{:T(128)}, s32[]{:T(128)}) %tuple.159), condition=%wide.region_13.14_spmd, body=%wide.region_12.13_spmd.sunk | while | flops 786437 | bytes 28311688 | solution.py:188
  774.3 3.3 bitcast_add_fusion.2
  777.6 8.8 dynamic_update_slice.45
  793.4 3.3 bitcast_add_fusion.2
  796.6 8.8 dynamic_update_slice.45
  812.4 3.3 bitcast_add_fusion.2
  815.7 8.8 dynamic_update_slice.45
  831.5 3.3 bitcast_add_fusion.2
  834.8 8.8 dynamic_update_slice.45
  843.5 3.3 convert.14
  849.8 11.5 %collective-permute-start.14 = (bf16[512,256]{1,0:T(8,128)(2,1)S(1)}, bf16[512,256]{1,0:T(8,128)(2,1)S(1)}, u32[]{:S(2)}, u32[]{:S(2)}) collective-permute-start(bf16[512,256]{1,0:T(8,128)(2,1)S(1)} %get-tuple-element.484), channel_id=1, source_target_pairs={{4,0},{5,1},{6,2},{7,3},{8,4},{9,5},{10,6},{11,7},{12,8},{13,9},{1... | collective-permute-start | bytes 786440 | tf_op jit(solution)/shard_map/ppermute | solution.py:16
  865.1 3.1 collective-permute-start.17
  870.3 6.8 collective-permute-start.19
  887.2 4.3 collective-permute-done.21
  891.5 18.8 %collective-permute-done.22 = bf16[512,256]{1,0:T(8,128)(2,1)S(1)} collective-permute-done((bf16[512,256]{1,0:T(8,128)(2,1)S(1)}, bf16[512,256]{1,0:T(8,128)(2,1)S(1)}, u32[]{:S(2)}, u32[]{:S(2)}) %collective-permute-start.22) | collective-permute-done | bytes 262176 | tf_op jit(solution)/shard_map/ppermute | solution.py:16
  910.3 6.0 collective-permute-done.23
  (931 shorter events, 628.3 us)
Async XLA Ops:
  0.6 15.8 %copy-start.2 = (bf16[512,1024]{1,0:T(8,128)(2,1)S(1)}, bf16[512,1024]{1,0:T(8,128)(2,1)}, u32[]{:S(2)}) copy-start(bf16[512,1024]{1,0:T(8,128)(2,1)} %param.14) | copy-start | bytes 3145732
  0.6 20.6 %collective-permute-start = (bf16[512,256]{1,0:T(8,128)(2,1)}, bf16[512,256]{1,0:T(8,128)(2,1)S(1)}, u32[]{:S(2)}, u32[]{:S(2)}) collective-permute-start(bf16[512,256]{1,0:T(8,128)(2,1)} %param.13), channel_id=1, source_target_pairs={{0,6},{1,7},{2,8},{3,9},{4,10},{5,11},{6,12},{7,13},{8,14},{9,15},... | collective-permute-start | bytes 786440 | tf_op jit(solution)/shard_map/ppermute | solution.py:16
  2.1 24.6 %collective-permute-start.1 = (bf16[512,256]{1,0:T(8,128)(2,1)}, bf16[512,256]{1,0:T(8,128)(2,1)}, u32[]{:S(2)}, u32[]{:S(2)}) collective-permute-start(bf16[512,256]{1,0:T(8,128)(2,1)} %param.13), channel_id=1, source_target_pairs={{0,5},{1,6},{2,7},{3,8},{4,9},{5,10},{6,11},{7,12},{8,13},{9,14},{... | collective-permute-start | bytes 786440 | tf_op jit(solution)/shard_map/ppermute | solution.py:16
  3.4 27.0 %collective-permute-start.2 = (bf16[512,256]{1,0:T(8,128)(2,1)}, bf16[512,256]{1,0:T(8,128)(2,1)}, u32[]{:S(2)}, u32[]{:S(2)}) collective-permute-start(bf16[512,256]{1,0:T(8,128)(2,1)} %param.13), channel_id=1, source_target_pairs={{0,4},{1,5},{2,6},{3,7},{4,8},{5,9},{6,10},{7,11},{8,12},{9,13},{1... | collective-permute-start | bytes 786440 | tf_op jit(solution)/shard_map/ppermute | solution.py:16
  4.7 31.3 %collective-permute-start.3 = (bf16[512,256]{1,0:T(8,128)(2,1)}, bf16[512,256]{1,0:T(8,128)(2,1)}, u32[]{:S(2)}, u32[]{:S(2)}) collective-permute-start(bf16[512,256]{1,0:T(8,128)(2,1)} %param.13), channel_id=1, source_target_pairs={{0,3},{1,4},{2,5},{3,6},{4,7},{5,8},{6,9},{7,10},{8,11},{9,12},{10... | collective-permute-start | bytes 786440 | tf_op jit(solution)/shard_map/ppermute | solution.py:16
  7.5 33.6 %collective-permute-start.4 = (bf16[512,256]{1,0:T(8,128)(2,1)}, bf16[512,256]{1,0:T(8,128)(2,1)}, u32[]{:S(2)}, u32[]{:S(2)}) collective-permute-start(bf16[512,256]{1,0:T(8,128)(2,1)} %param.13), channel_id=1, source_target_pairs={{0,2},{1,3},{2,4},{3,5},{4,6},{5,7},{6,8},{7,9},{8,10},{9,11},{10,... | collective-permute-start | bytes 786440 | tf_op jit(solution)/shard_map/ppermute | solution.py:16
  21.9 25.4 %collective-permute-start.5 = (bf16[512,256]{1,0:T(8,128)(2,1)}, bf16[512,256]{1,0:T(8,128)(2,1)S(1)}, u32[]{:S(2)}, u32[]{:S(2)}) collective-permute-start(bf16[512,256]{1,0:T(8,128)(2,1)} %param.13), channel_id=1, source_target_pairs={{0,1},{1,2},{2,3},{3,4},{4,5},{5,6},{6,7},{7,8},{8,9},{9,10},{10,1... | collective-permute-start | bytes 786440 | tf_op jit(solution)/shard_map/ppermute | solution.py:16
  26.7 22.9 %collective-permute-start.6 = (bf16[512,256]{1,0:T(8,128)(2,1)}, bf16[512,256]{1,0:T(8,128)(2,1)S(1)}, u32[]{:S(2)}, u32[]{:S(2)}) collective-permute-start(bf16[512,256]{1,0:T(8,128)(2,1)} %param.13), channel_id=1, source_target_pairs={{1,0},{2,1},{3,2},{4,3},{5,4},{6,5},{7,6},{8,7},{9,8},{10,9},{11,1... | collective-permute-start | bytes 786440 | tf_op jit(solution)/shard_map/ppermute | solution.py:16
  30.4 20.8 %collective-permute-start.7 = (bf16[512,256]{1,0:T(8,128)(2,1)}, bf16[512,256]{1,0:T(8,128)(2,1)S(1)}, u32[]{:S(2)}, u32[]{:S(2)}) collective-permute-start(bf16[512,256]{1,0:T(8,128)(2,1)} %param.13), channel_id=1, source_target_pairs={{2,0},{3,1},{4,2},{5,3},{6,4},{7,5},{8,6},{9,7},{10,8},{11,9},{12,... | collective-permute-start | bytes 786440 | tf_op jit(solution)/shard_map/ppermute | solution.py:16
  36.0 15.2 %collective-permute-start.8 = (bf16[512,256]{1,0:T(8,128)(2,1)}, bf16[512,256]{1,0:T(8,128)(2,1)S(1)}, u32[]{:S(2)}, u32[]{:S(2)}) collective-permute-start(bf16[512,256]{1,0:T(8,128)(2,1)} %param.13), channel_id=1, source_target_pairs={{3,0},{4,1},{5,2},{6,3},{7,4},{8,5},{9,6},{10,7},{11,8},{12,9},{13... | collective-permute-start | bytes 786440 | tf_op jit(solution)/shard_map/ppermute | solution.py:16
  41.1 12.2 %collective-permute-start.9 = (bf16[512,256]{1,0:T(8,128)(2,1)}, bf16[512,256]{1,0:T(8,128)(2,1)S(1)}, u32[]{:S(2)}, u32[]{:S(2)}) collective-permute-start(bf16[512,256]{1,0:T(8,128)(2,1)} %param.13), channel_id=1, source_target_pairs={{4,0},{5,1},{6,2},{7,3},{8,4},{9,5},{10,6},{11,7},{12,8},{13,9},{1... | collective-permute-start | bytes 786440 | tf_op jit(solution)/shard_map/ppermute | solution.py:16
  47.3 11.7 %collective-permute-start.10 = (bf16[512,256]{1,0:T(8,128)(2,1)}, bf16[512,256]{1,0:T(8,128)(2,1)S(1)}, u32[]{:S(2)}, u32[]{:S(2)}) collective-permute-start(bf16[512,256]{1,0:T(8,128)(2,1)} %param.13), channel_id=1, source_target_pairs={{5,0},{6,1},{7,2},{8,3},{9,4},{10,5},{11,6},{12,7},{13,8},{14,9},{... | collective-permute-start | bytes 786440 | tf_op jit(solution)/shard_map/ppermute | solution.py:16
  49.6 14.1 %collective-permute-start.11 = (bf16[512,256]{1,0:T(8,128)(2,1)}, bf16[512,256]{1,0:T(8,128)(2,1)S(1)}, u32[]{:S(2)}, u32[]{:S(2)}) collective-permute-start(bf16[512,256]{1,0:T(8,128)(2,1)} %param.13), channel_id=1, source_target_pairs={{6,0},{7,1},{8,2},{9,3},{10,4},{11,5},{12,6},{13,7},{14,8},{15,9},... | collective-permute-start | bytes 786440 | tf_op jit(solution)/shard_map/ppermute | solution.py:16
  76.0 15.8 %copy-start = (bf16[1,256,512]{1,2,0:T(8,128)(2,1)}, bf16[1,256,512]{1,2,0:T(8,128)(2,1)S(1)}, u32[]{:S(2)}) copy-start(bf16[1,256,512]{1,2,0:T(8,128)(2,1)S(1)} %get-tuple-element.745) | copy-start | bytes 786436 | tf_op jit(solution)/shard_map/while
  162.0 1.0 copy-start.1
  176.9 1.0 copy-start.1
  184.3 1.0 copy-start.1
  199.1 1.0 copy-start.1
  206.5 1.0 copy-start.1
  214.0 1.0 copy-start.1
  221.4 1.0 copy-start.1
  236.2 1.0 copy-start.1
  248.3 15.8 %copy-start = (bf16[1,256,512]{1,2,0:T(8,128)(2,1)}, bf16[1,256,512]{1,2,0:T(8,128)(2,1)S(1)}, u32[]{:S(2)}) copy-start(bf16[1,256,512]{1,2,0:T(8,128)(2,1)S(1)} %get-tuple-element.745) | copy-start | bytes 786436 | tf_op jit(solution)/shard_map/while
  326.9 1.0 copy-start.1
  341.7 1.0 copy-start.1
  363.9 1.0 copy-start.1
  378.8 1.0 copy-start.1
  386.2 1.0 copy-start.1
  401.0 1.0 copy-start.1
  408.5 1.0 copy-start.1
  420.5 15.8 %copy-start = (bf16[1,256,512]{1,2,0:T(8,128)(2,1)}, bf16[1,256,512]{1,2,0:T(8,128)(2,1)S(1)}, u32[]{:S(2)}) copy-start(bf16[1,256,512]{1,2,0:T(8,128)(2,1)S(1)} %get-tuple-element.745) | copy-start | bytes 786436 | tf_op jit(solution)/shard_map/while
  499.2 1.0 copy-start.1
  514.0 1.0 copy-start.1
  592.9 15.8 %copy-start = (bf16[1,256,512]{1,2,0:T(8,128)(2,1)}, bf16[1,256,512]{1,2,0:T(8,128)(2,1)S(1)}, u32[]{:S(2)}) copy-start(bf16[1,256,512]{1,2,0:T(8,128)(2,1)S(1)} %get-tuple-element.745) | copy-start | bytes 786436 | tf_op jit(solution)/shard_map/while
  764.1 3.2 copy-start.5
  846.8 38.1 %copy-start.3 = (bf16[4,256,512]{2,1,0:T(8,128)(2,1)S(1)}, bf16[4,256,512]{2,1,0:T(8,128)(2,1)}, u32[]{:S(2)}) copy-start(bf16[4,256,512]{2,1,0:T(8,128)(2,1)} %get-tuple-element.322) | copy-start | bytes 3145732
  847.0 18.1 %collective-permute-start.12 = (bf16[512,256]{1,0:T(8,128)(2,1)S(1)}, bf16[512,256]{1,0:T(8,128)(2,1)S(1)}, u32[]{:S(2)}, u32[]{:S(2)}) collective-permute-start(bf16[512,256]{1,0:T(8,128)(2,1)S(1)} %get-tuple-element.474), channel_id=1, source_target_pairs={{6,0},{7,1},{8,2},{9,3},{10,4},{11,5},{12,6},{13,7},{14,8},{15,9},... | collective-permute-start | bytes 786440 | tf_op jit(solution)/shard_map/ppermute | solution.py:16
  848.5 19.8 %collective-permute-start.13 = (bf16[512,256]{1,0:T(8,128)(2,1)S(1)}, bf16[512,256]{1,0:T(8,128)(2,1)S(1)}, u32[]{:S(2)}, u32[]{:S(2)}) collective-permute-start(bf16[512,256]{1,0:T(8,128)(2,1)S(1)} %get-tuple-element.485), channel_id=1, source_target_pairs={{5,0},{6,1},{7,2},{8,3},{9,4},{10,5},{11,6},{12,7},{13,8},{14,9},{... | collective-permute-start | bytes 786440 | tf_op jit(solution)/shard_map/ppermute | solution.py:16
  849.8 20.5 %collective-permute-start.14 = (bf16[512,256]{1,0:T(8,128)(2,1)S(1)}, bf16[512,256]{1,0:T(8,128)(2,1)S(1)}, u32[]{:S(2)}, u32[]{:S(2)}) collective-permute-start(bf16[512,256]{1,0:T(8,128)(2,1)S(1)} %get-tuple-element.484), channel_id=1, source_target_pairs={{4,0},{5,1},{6,2},{7,3},{8,4},{9,5},{10,6},{11,7},{12,8},{13,9},{1... | collective-permute-start | bytes 786440 | tf_op jit(solution)/shard_map/ppermute | solution.py:16
  861.3 15.8 %collective-permute-start.15 = (bf16[512,256]{1,0:T(8,128)(2,1)S(1)}, bf16[512,256]{1,0:T(8,128)(2,1)S(1)}, u32[]{:S(2)}, u32[]{:S(2)}) collective-permute-start(bf16[512,256]{1,0:T(8,128)(2,1)S(1)} %get-tuple-element.483), channel_id=1, source_target_pairs={{3,0},{4,1},{5,2},{6,3},{7,4},{8,5},{9,6},{10,7},{11,8},{12,9},{13... | collective-permute-start | bytes 786440 | tf_op jit(solution)/shard_map/ppermute | solution.py:16
  863.2 16.1 %collective-permute-start.16 = (bf16[512,256]{1,0:T(8,128)(2,1)S(1)}, bf16[512,256]{1,0:T(8,128)(2,1)S(1)}, u32[]{:S(2)}, u32[]{:S(2)}) collective-permute-start(bf16[512,256]{1,0:T(8,128)(2,1)S(1)} %get-tuple-element.482), channel_id=1, source_target_pairs={{2,0},{3,1},{4,2},{5,3},{6,4},{7,5},{8,6},{9,7},{10,8},{11,9},{12,... | collective-permute-start | bytes 786440 | tf_op jit(solution)/shard_map/ppermute | solution.py:16
  865.1 17.2 %collective-permute-start.17 = (bf16[512,256]{1,0:T(8,128)(2,1)S(1)}, bf16[512,256]{1,0:T(8,128)(2,1)S(1)}, u32[]{:S(2)}, u32[]{:S(2)}) collective-permute-start(bf16[512,256]{1,0:T(8,128)(2,1)S(1)} %get-tuple-element.481), channel_id=1, source_target_pairs={{1,0},{2,1},{3,2},{4,3},{5,4},{6,5},{7,6},{8,7},{9,8},{10,9},{11,1... | collective-permute-start | bytes 786440 | tf_op jit(solution)/shard_map/ppermute | solution.py:16
  868.2 15.4 %collective-permute-start.18 = (bf16[512,256]{1,0:T(8,128)(2,1)S(1)}, bf16[512,256]{1,0:T(8,128)(2,1)S(1)}, u32[]{:S(2)}, u32[]{:S(2)}) collective-permute-start(bf16[512,256]{1,0:T(8,128)(2,1)S(1)} %get-tuple-element.480), channel_id=1, source_target_pairs={{0,1},{1,2},{2,3},{3,4},{4,5},{5,6},{6,7},{7,8},{8,9},{9,10},{10,1... | collective-permute-start | bytes 786440 | tf_op jit(solution)/shard_map/ppermute | solution.py:16
  870.3 17.0 %collective-permute-start.19 = (bf16[512,256]{1,0:T(8,128)(2,1)S(1)}, bf16[512,256]{1,0:T(8,128)(2,1)S(1)}, u32[]{:S(2)}, u32[]{:S(2)}) collective-permute-start(bf16[512,256]{1,0:T(8,128)(2,1)S(1)} %get-tuple-element.479), channel_id=1, source_target_pairs={{0,2},{1,3},{2,4},{3,5},{4,6},{5,7},{6,8},{7,9},{8,10},{9,11},{10,... | collective-permute-start | bytes 786440 | tf_op jit(solution)/shard_map/ppermute | solution.py:16
  877.1 10.2 %collective-permute-start.20 = (bf16[512,256]{1,0:T(8,128)(2,1)S(1)}, bf16[512,256]{1,0:T(8,128)(2,1)S(1)}, u32[]{:S(2)}, u32[]{:S(2)}) collective-permute-start(bf16[512,256]{1,0:T(8,128)(2,1)S(1)} %get-tuple-element.478), channel_id=1, source_target_pairs={{0,3},{1,4},{2,5},{3,6},{4,7},{5,8},{6,9},{7,10},{8,11},{9,12},{10... | collective-permute-start | bytes 786440 | tf_op jit(solution)/shard_map/ppermute | solution.py:16
  879.3 12.2 %collective-permute-start.21 = (bf16[512,256]{1,0:T(8,128)(2,1)S(1)}, bf16[512,256]{1,0:T(8,128)(2,1)S(1)}, u32[]{:S(2)}, u32[]{:S(2)}) collective-permute-start(bf16[512,256]{1,0:T(8,128)(2,1)S(1)} %get-tuple-element.477), channel_id=1, source_target_pairs={{0,4},{1,5},{2,6},{3,7},{4,8},{5,9},{6,10},{7,11},{8,12},{9,13},{1... | collective-permute-start | bytes 786440 | tf_op jit(solution)/shard_map/ppermute | solution.py:16
  882.3 28.0 %collective-permute-start.22 = (bf16[512,256]{1,0:T(8,128)(2,1)S(1)}, bf16[512,256]{1,0:T(8,128)(2,1)S(1)}, u32[]{:S(2)}, u32[]{:S(2)}) collective-permute-start(bf16[512,256]{1,0:T(8,128)(2,1)S(1)} %get-tuple-element.476), channel_id=1, source_target_pairs={{0,5},{1,6},{2,7},{3,8},{4,9},{5,10},{6,11},{7,12},{8,13},{9,14},{... | collective-permute-start | bytes 786440 | tf_op jit(solution)/shard_map/ppermute | solution.py:16
  883.6 32.7 %collective-permute-start.23 = (bf16[512,256]{1,0:T(8,128)(2,1)S(1)}, bf16[512,256]{1,0:T(8,128)(2,1)S(1)}, u32[]{:S(2)}, u32[]{:S(2)}) collective-permute-start(bf16[512,256]{1,0:T(8,128)(2,1)S(1)} %get-tuple-element.475), channel_id=1, source_target_pairs={{0,6},{1,7},{2,8},{3,9},{4,10},{5,11},{6,12},{7,13},{8,14},{9,15},... | collective-permute-start | bytes 786440 | tf_op jit(solution)/shard_map/ppermute | solution.py:16
  (32 other events, 30.2 us)
where the time goes:
time: 932 us; the launch traced here: 919 us
  local copies, waits for them, and re-layouts  395 us (42%)
  matrix products  245 us (26%)
  loops' own time  84.8 us (9%)
  other arithmetic  79.5 us (9%)
  starting transfers between devices  65.9 us (7%)
  waiting for transfers between devices  47.3 us (5%)
    dot_general x48, matrix products, second_pass(): jnp.einsum('rgk,kc->rgc', grad_scores, key_block, preferred_element_type=...  104 us
    dynamic_slice x96, local copies, waits for them, and re-layouts, fetch(): lax.dynamic_index_in_dim(prob_store, block_index, 0, keepdims=False)  101 us
    dynamic_update_slice x48, local copies, waits for them, and re-layouts, first_pass(): lax.dynamic_update_index_in_dim(prob_store, grad_probs, block_index, 0)  76.4 us
    ppermute x24, starting transfers between devices, passed_along(): lax.ppermute(value, axis, [(source, source + steps) for source in range(i...  65.9 us
    another operation x28, local copies, waits for them, and re-layouts  60.6 us
    dot_general x48, matrix products, block_scores(): jnp.einsum('rgc,kc->rgk', grad_block, value_block, preferred_element_type...  56.2 us
    dot_general x48, matrix products, block_scores(): jnp.einsum('rgc,kc->rgk', query_block, key_block, preferred_element_type=...  55.4 us
    ppermute x24, waiting for transfers between devices, passed_along(): lax.ppermute(value, axis, [(source, source + steps) for source in range(i...  47.3 us
  transfers between devices with their start and end apart: 24, of which 10 were waited for; matrix products, arithmetic and copies ran while one was open for 2% of the time, Pallas kernels for 0%

commit v1 on v0

v1 whole, which is shorter than its diff:
```python
import functools

import jax
import jax.numpy as jnp
from jax import lax
from jax.experimental import pallas as pl
from jax.experimental.pallas import tpu as pltpu
from jax.sharding import PartitionSpec as P

HD = 128
QH = 8
HG = 4
TILE = 256
MOST = 12
STEP = 2
SCALE = HD**-0.5
SCALE_LOG2 = SCALE * 1.4426950408889634
F32 = jnp.float32
BF16 = jnp.bfloat16


def attention_kernel(
    reach, per_device, lengths, own_any, twin_any, q_ref, g_ref, dq_ref, own_out, twin_out,
    kv, acc, low, exps, gprobs, maxes, keys_t, q_t, g_t, dq_t, in_sems, out_sems,
):
    pieces = 2 * reach + 1
    rows_dev = per_device * TILE
    me = lax.axis_index("dp")
    core = lax.rem(me, 2)
    base_tile = (me // 2 - reach) * 2 * per_device

    def near(piece, which):
        return pl.ds(pl.multiple_of((piece * 2 + which) * rows_dev, rows_dev), rows_dev)

    def far(piece):
        return pl.ds(piece * rows_dev, rows_dev)

    loads = []
    for piece in range(pieces):
        for side, (source, which) in enumerate(((own_any, core), (twin_any, 1 - core))):
            loads.append(
                pltpu.make_async_copy(
                    source.at[far(piece)], kv.at[near(piece, which)], in_sems.at[side, piece]
                )
            )
    for load in loads:
        load.start()
    acc[...] = jnp.zeros_like(acc)
    for load in loads:
        load.wait()

    groups = QH // HG

    def unit(index, _):
        tile = index // groups
        group = index % groups
        own_tile = me * per_device + tile
        first = jnp.int32(0)
        count = jnp.int32(0)
        end = jnp.int32(0)
        for pair in range(lengths.shape[0]):
            start = end
            size = lengths[pair]
            end = start + size
            inside = (own_tile >= start) & (own_tile < end)
            first = jnp.where(inside, start, first)
            count = jnp.where(inside, size, count)
        first = first - base_tile
        rows = pl.ds(pl.multiple_of(tile * TILE, TILE), TILE)

        def cols(head):
            return pl.ds(pl.multiple_of((group * HG + head) * HD, HD), HD)

        def kv_rows(block, blocks):
            return pl.ds(pl.multiple_of((first + block) * TILE, TILE), blocks * TILE)

        def local(block, blocks):
            return pl.ds(pl.multiple_of(block * TILE, TILE), blocks * TILE)

        @pl.when(group == 0)
        def _():
            def turn(block, _):
                keys_t[:, local(block, 1)] = kv[kv_rows(block, 1), :HD].T
                return 0

            lax.fori_loop(0, count, turn, 0)

        for head in range(HG):
            q_t[head] = q_ref[rows, cols(head)].T
            g_t[head] = g_ref[rows, cols(head)].T

        def sweep(step, state):
            whole = count // STEP
            state = lax.fori_loop(0, whole, lambda i, s: step(i * STEP, STEP, s), state)
            return lax.fori_loop(whole * STEP, count, lambda b, s: step(b, 1, s), state)

        def scores(block, blocks, state):
            at, here = kv_rows(block, blocks), local(block, blocks)
            done = []
            for head in range(HG):
                top, total, weighted = state[head]
                score = jnp.dot(kv[at, :HD], q_t[head], preferred_element_type=F32)
                gprob = jnp.dot(kv[at, HD:], g_t[head], preferred_element_type=F32)
                new_top = jnp.maximum(top, jnp.max(score, axis=0, keepdims=True))
                gprobs[head, here] = gprob
                weight = jnp.exp2((score - new_top) * SCALE_LOG2)
                fade = jnp.exp2((top - new_top) * SCALE_LOG2)
                total = total * fade + jnp.sum(weight, axis=0, keepdims=True)
                weighted = weighted * fade + jnp.sum(weight * gprob, axis=0, keepdims=True)
                exps[head, here] = weight
                maxes[head, block] = new_top
                done.append((new_top, total, weighted))
            return tuple(done)

        zero = jnp.zeros((1, TILE), F32)
        state = sweep(scores, tuple((jnp.full((1, TILE), -jnp.inf, F32), zero, zero) for _ in range(HG)))
        stats = tuple((top, 1.0 / total, weighted / total) for top, total, weighted in state)
        dq_t[...] = jnp.zeros_like(dq_t)

        def grads(block, blocks, _):
            at, here = kv_rows(block, blocks), local(block, blocks)
            key_t = keys_t[:, here]
            for head in range(HG):
                top, inverse, delta = stats[head]
                factor = jnp.exp2((maxes[head, block] - top) * SCALE_LOG2) * inverse
                prob = exps[head, here] * factor
                dscore = (prob * (gprobs[head, here] - delta)).astype(BF16)
                prob = prob.astype(BF16)
                dq_t[head] += jnp.dot(key_t, dscore, preferred_element_type=F32)
                acc[at, :HD] += jnp.dot(dscore, q_ref[rows, cols(head)], preferred_element_type=F32) * SCALE
                acc[at, HD:] += jnp.dot(prob, g_ref[rows, cols(head)], preferred_element_type=F32)
            return 0

        sweep(grads, 0)
        for head in range(HG):
            dq_ref[rows, cols(head)] = (dq_t[head] * SCALE).T.astype(BF16)
        return 0

    lax.fori_loop(0, per_device * groups, unit, 0)

    stores = []
    for piece in range(pieces):
        stores.append(
            pltpu.make_async_copy(acc.at[near(piece, core)], own_out.at[far(piece)], out_sems.at[0, piece])
        )
        stores[-1].start()
    low[...] = acc[...].astype(BF16)
    for piece in range(pieces):
        stores.append(
            pltpu.make_async_copy(low.at[near(piece, 1 - core)], twin_out.at[far(piece)], out_sems.at[1, piece])
        )
        stores[-1].start()
    for store in stores:
        store.wait()


def attention(reach, lengths, own, twin, queries, grad_out):
    pieces = 2 * reach + 1
    rows_dev = queries.shape[0]
    per_device = rows_dev // TILE
    near_rows = 2 * pieces * rows_dev
    vmem = pl.BlockSpec(memory_space=pltpu.VMEM)
    hbm = pl.BlockSpec(memory_space=pl.ANY)
    return pl.pallas_call(
        functools.partial(attention_kernel, reach, per_device),
        out_shape=(
            jax.ShapeDtypeStruct(queries.shape, BF16),
            jax.ShapeDtypeStruct((pieces * rows_dev, 2 * HD), F32),
            jax.ShapeDtypeStruct((pieces * rows_dev, 2 * HD), BF16),
        ),
        in_specs=[pl.BlockSpec(memory_space=pltpu.SMEM), hbm, hbm, vmem, vmem],
        out_specs=(vmem, hbm, hbm),
        scratch_shapes=[
            pltpu.VMEM((near_rows, 2 * HD), BF16),
            pltpu.VMEM((near_rows, 2 * HD), F32),
            pltpu.VMEM((near_rows, 2 * HD), BF16),
            pltpu.VMEM((HG, MOST * TILE, TILE), F32),
            pltpu.VMEM((HG, MOST * TILE, TILE), F32),
            pltpu.VMEM((HG, MOST, 1, TILE), F32),
            pltpu.VMEM((HD, MOST * TILE), BF16),
            pltpu.VMEM((HG, HD, TILE), BF16),
            pltpu.VMEM((HG, HD, TILE), BF16),
            pltpu.VMEM((HG, HD, TILE), F32),
            pltpu.SemaphoreType.DMA((2, pieces)),
            pltpu.SemaphoreType.DMA((2, pieces)),
        ],
        compiler_params=pltpu.CompilerParams(vmem_limit_bytes=60 * 2**20),
    )(lengths, own, twin, queries, grad_out)


def body(queries, kv_cache, grad_out, pair_lengths):
    rows_dev = queries.shape[0]
    per_chip = 2 * rows_dev // TILE
    reach = (MOST - 1 + per_chip - 1) // per_chip
    count = lax.axis_size("dp")

    def by_chips(value, chips):
        steps = 2 * chips
        return lax.ppermute(
            value, "dp", [(i, i + steps) for i in range(count) if 0 <= i + steps < count]
        )

    def to_twin(value):
        return lax.ppermute(value, "dp", [(i, i ^ 1) for i in range(count)])

    own = jnp.concatenate(
        [kv_cache if chips == 0 else by_chips(kv_cache, -chips) for chips in range(-reach, reach + 1)], axis=0
    )
    twin = to_twin(own)
    grad_queries, own_grad, twin_grad = attention(reach, pair_lengths, own, twin, queries, grad_out)
    summed = own_grad + to_twin(twin_grad).astype(F32)
    grad_kv = summed[reach * rows_dev : (reach + 1) * rows_dev]
    for chips in range(-reach, reach + 1):
        if chips != 0:
            low = (chips + reach) * rows_dev
            grad_kv = grad_kv + by_chips(summed[low : low + rows_dev].astype(BF16), chips).astype(F32)
    return grad_queries, grad_kv


def solution(mesh):
    tokens = P(("groups", "dp"), None)
    return jax.shard_map(
        body,
        mesh=mesh,
        in_specs=(tokens, tokens, tokens, P("groups")),
        out_specs=(tokens, tokens),
        check_vma=False,
    )
```

time: 932 us -> 139 us (0.15)
  the two profiles are of different devices: /device:TPU:26 before, /device:TPU:0 now
where the time goes in v1:
time: 139 us
  starting transfers between devices  83.3 us (60%)
  waiting for transfers between devices  31.9 us (23%)
  Pallas kernels  17 us (12%)
  other arithmetic  3.6 us (3%)
  local copies, waits for them, and re-layouts  2.44 us (2%)
    ppermute x12, starting transfers between devices, by_chips(): lax.ppermute(value, 'dp', [(i, i + steps) for i in range(count) if 0 <= i...  78.3 us
    ppermute x12, waiting for transfers between devices, by_chips(): lax.ppermute(value, 'dp', [(i, i + steps) for i in range(count) if 0 <= i...  24.5 us
    pallas_call x1, Pallas kernels, attention(): pl.pallas_call(functools.partial(attention_kernel, reach, per_device), ou...  17 us
    ppermute x2, waiting for transfers between devices, to_twin(): return lax.ppermute(value, 'dp', [(i, i ^ 1) for i in range(count)])  7.39 us
    ppermute x2, starting transfers between devices, to_twin(): return lax.ppermute(value, 'dp', [(i, i ^ 1) for i in range(count)])  4.94 us
  transfers between devices with their start and end apart: 14, of which 8 were waited for; matrix products, arithmetic and copies ran while one was open for 1% of the time, Pallas kernels for 0%

profile of v1, /device:TPU:0, one launch (start us, length us, event | category | flops | bytes accessed | tf_op | source)
XLA Modules:
  0.0 139.1 jit_solution(6720833746999762197)
XLA Ops:
  0.6 5.9 %collective-permute-start = (bf16[512,256]{1,0:T(8,128)(2,1)}, bf16[512,256]{1,0:T(8,128)(2,1)S(1)}, u32[]{:S(2)}, u32[]{:S(2)}) collective-permute-start(bf16[512,256]{1,0:T(8,128)(2,1)} %param.5), channel_id=1, source_target_pairs={{0,6},{1,7},{2,8},{3,9},{4,10},{5,11},{6,12},{7,13},{8,14},{9,15},... | collective-permute-start | bytes 786440 | tf_op jit(solution)/shard_map/ppermute | solution.py:199
  6.5 3.5 %collective-permute-start.1 = (bf16[512,256]{1,0:T(8,128)(2,1)}, bf16[512,256]{1,0:T(8,128)(2,1)S(1)}, u32[]{:S(2)}, u32[]{:S(2)}) collective-permute-start(bf16[512,256]{1,0:T(8,128)(2,1)} %param.5), channel_id=1, source_target_pairs={{0,4},{1,5},{2,6},{3,7},{4,8},{5,9},{6,10},{7,11},{8,12},{9,13},{1... | collective-permute-start | bytes 786440 | tf_op jit(solution)/shard_map/ppermute | solution.py:199
  10.0 3.4 %collective-permute-start.2 = (bf16[512,256]{1,0:T(8,128)(2,1)}, bf16[512,256]{1,0:T(8,128)(2,1)S(1)}, u32[]{:S(2)}, u32[]{:S(2)}) collective-permute-start(bf16[512,256]{1,0:T(8,128)(2,1)} %param.5), channel_id=1, source_target_pairs={{0,2},{1,3},{2,4},{3,5},{4,6},{5,7},{6,8},{7,9},{8,10},{9,11},{10,... | collective-permute-start | bytes 786440 | tf_op jit(solution)/shard_map/ppermute | solution.py:199
  13.5 1.3 collective-permute-start.4
  14.8 1.3 collective-permute-start.3
  16.1 0.0 collective-permute-done
  16.1 1.3 collective-permute-start.5
  17.4 0.6 collective-permute-done.1
  18.0 0.7 collective-permute-done.2
  18.8 1.0 constant_dynamic-update-slice_fusion.3
  19.8 9.9 %collective-permute-done.3 = bf16[512,256]{1,0:T(8,128)(2,1)S(1)} collective-permute-done((bf16[512,256]{1,0:T(8,128)(2,1)}, bf16[512,256]{1,0:T(8,128)(2,1)S(1)}, u32[]{:S(2)}, u32[]{:S(2)}) %collective-permute-start.3) | collective-permute-done | bytes 262176 | tf_op jit(solution)/shard_map/ppermute | solution.py:199
  29.7 0.0 collective-permute-done.4
  29.8 0.0 collective-permute-done.5
  29.8 0.0 copy-start
  29.8 0.1 collective-permute-start.6
  29.9 3.8 %collective-permute-done.6.twin_any = bf16[3584,256]{1,0:T(8,128)(2,1)S(1)} collective-permute-done((bf16[3584,256]{1,0:T(8,128)(2,1)S(1)}, bf16[3584,256]{1,0:T(8,128)(2,1)S(1)}, u32[]{:S(2)}, u32[]{:S(2)}) %collective-permute-start.6) | collective-permute-done | bytes 1835040 | tf_op jit(solution)/shard_map/ppermute | solution.py:204
  33.7 0.0 copy-done
  33.7 0.0 copy-start.1
  33.7 1.2 copy-done.1
  34.9 17.0 %shard_map.59 = (bf16[512,1024]{1,0:T(8,128)(2,1)}, f32[3584,256]{1,0:T(8,128)}, bf16[3584,256]{1,0:T(8,128)(2,1)}) custom-call(s32[10]{0:T(128)} %lengths.1, bf16[3584,256]{1,0:T(8,128)(2,1)} %copy-done, bf16[3584,256]{1,0:T(8,128)(2,1)} %copy-done.1, bf16[512,1024]{1,0:T(8,128)(2,1)} %q_ref.1, bf16[512,1024]{1,0:T(8,128)(2,1)} %g_ref.1), custom_call_target="tpu_custom_call" | custom-call | tf_op jit(solution)/shard_map/pallas_call | solution.py:164
  52.0 4.9 %collective-permute-start.7 = (bf16[3584,256]{1,0:T(8,128)(2,1)}, bf16[3584,256]{1,0:T(8,128)(2,1)S(1)}, u32[]{:S(2)}, u32[]{:S(2)}) collective-permute-start(bf16[3584,256]{1,0:T(8,128)(2,1)} %get-tuple-element.7), channel_id=1, source_target_pairs={{0,1},{1,0},{2,3},{3,2},{4,5},{5,4},{6,7},{7,6},{8,9},{9,8},{10,11... | collective-permute-start | bytes 5505032 | tf_op jit(solution)/shard_map/ppermute | solution.py:204
  56.8 3.6 %collective-permute-done.7 = bf16[3584,256]{1,0:T(8,128)(2,1)S(1)} collective-permute-done((bf16[3584,256]{1,0:T(8,128)(2,1)}, bf16[3584,256]{1,0:T(8,128)(2,1)S(1)}, u32[]{:S(2)}, u32[]{:S(2)}) %collective-permute-start.7) | collective-permute-done | bytes 1835040 | tf_op jit(solution)/shard_map/ppermute | solution.py:204
  60.5 2.6 %fusion.5 = (bf16[3584,256]{1,0:T(8,128)(2,1)S(1)}, f32[3584,256]{1,0:T(8,128)S(1)}) fusion(f32[3584,256]{1,0:T(8,128)} %get-tuple-element.6, bf16[3584,256]{1,0:T(8,128)(2,1)S(1)} %collective-permute-done.7), kind=kLoop, calls=%fused_computation.14 | loop fusion | flops 2752512 | bytes 11010048 | tf_op jit(solution)/shard_map/convert.5
  63.0 0.1 fusion.6
  63.2 1.3 collective-permute-start.8
  64.5 46.7 %collective-permute-start.13 = (bf16[512,256]{1,0:T(8,128)(2,1)S(1)}, bf16[512,256]{1,0:T(8,128)(2,1)S(1)}, u32[]{:S(2)}, u32[]{:S(2)}) collective-permute-start(bf16[512,256]{1,0:T(8,128)(2,1)S(1)} %get-tuple-element.11), channel_id=1, source_target_pairs={{0,6},{1,7},{2,8},{3,9},{4,10},{5,11},{6,12},{7,13},{8,14},{9,15},... | collective-permute-start | bytes 786440 | tf_op jit(solution)/shard_map/ppermute | solution.py:199
  111.1 5.7 %collective-permute-start.12 = (bf16[512,256]{1,0:T(8,128)(2,1)S(1)}, bf16[512,256]{1,0:T(8,128)(2,1)S(1)}, u32[]{:S(2)}, u32[]{:S(2)}) collective-permute-start(bf16[512,256]{1,0:T(8,128)(2,1)S(1)} %get-tuple-element.12), channel_id=1, source_target_pairs={{0,4},{1,5},{2,6},{3,7},{4,8},{5,9},{6,10},{7,11},{8,12},{9,13},{1... | collective-permute-start | bytes 786440 | tf_op jit(solution)/shard_map/ppermute | solution.py:199
  116.8 5.4 %collective-permute-start.11 = (bf16[512,256]{1,0:T(8,128)(2,1)S(1)}, bf16[512,256]{1,0:T(8,128)(2,1)S(1)}, u32[]{:S(2)}, u32[]{:S(2)}) collective-permute-start(bf16[512,256]{1,0:T(8,128)(2,1)S(1)} %get-tuple-element.13), channel_id=1, source_target_pairs={{0,2},{1,3},{2,4},{3,5},{4,6},{5,7},{6,8},{7,9},{8,10},{9,11},{10,... | collective-permute-start | bytes 786440 | tf_op jit(solution)/shard_map/ppermute | solution.py:199
  122.2 1.3 collective-permute-start.10
  123.5 0.0 collective-permute-done.8
  123.5 1.3 collective-permute-start.9
  124.8 0.0 collective-permute-done.13
  124.9 2.3 %collective-permute-done.12 = bf16[512,256]{1,0:T(8,128)(2,1)S(1)} collective-permute-done((bf16[512,256]{1,0:T(8,128)(2,1)S(1)}, bf16[512,256]{1,0:T(8,128)(2,1)S(1)}, u32[]{:S(2)}, u32[]{:S(2)}) %collective-permute-start.12) | collective-permute-done | bytes 262176 | tf_op jit(solution)/shard_map/ppermute | solution.py:199
  127.1 7.7 %collective-permute-done.11 = bf16[512,256]{1,0:T(8,128)(2,1)S(1)} collective-permute-done((bf16[512,256]{1,0:T(8,128)(2,1)S(1)}, bf16[512,256]{1,0:T(8,128)(2,1)S(1)}, u32[]{:S(2)}, u32[]{:S(2)}) %collective-permute-start.11) | collective-permute-done | bytes 262176 | tf_op jit(solution)/shard_map/ppermute | solution.py:199
  134.8 0.0 collective-permute-done.10
  134.8 3.3 %collective-permute-done.9 = bf16[512,256]{1,0:T(8,128)(2,1)S(1)} collective-permute-done((bf16[512,256]{1,0:T(8,128)(2,1)S(1)}, bf16[512,256]{1,0:T(8,128)(2,1)S(1)}, u32[]{:S(2)}, u32[]{:S(2)}) %collective-permute-start.9) | collective-permute-done | bytes 262176 | tf_op jit(solution)/shard_map/ppermute | solution.py:199
  138.1 1.0 fusion.4
  (6 shorter events, 0.1 us)
Async XLA Ops:
  0.6 15.5 %collective-permute-start = (bf16[512,256]{1,0:T(8,128)(2,1)}, bf16[512,256]{1,0:T(8,128)(2,1)S(1)}, u32[]{:S(2)}, u32[]{:S(2)}) collective-permute-start(bf16[512,256]{1,0:T(8,128)(2,1)} %param.5), channel_id=1, source_target_pairs={{0,6},{1,7},{2,8},{3,9},{4,10},{5,11},{6,12},{7,13},{8,14},{9,15},... | collective-permute-start | bytes 786440 | tf_op jit(solution)/shard_map/ppermute | solution.py:199
  6.5 11.5 %collective-permute-start.1 = (bf16[512,256]{1,0:T(8,128)(2,1)}, bf16[512,256]{1,0:T(8,128)(2,1)S(1)}, u32[]{:S(2)}, u32[]{:S(2)}) collective-permute-start(bf16[512,256]{1,0:T(8,128)(2,1)} %param.5), channel_id=1, source_target_pairs={{0,4},{1,5},{2,6},{3,7},{4,8},{5,9},{6,10},{7,11},{8,12},{9,13},{1... | collective-permute-start | bytes 786440 | tf_op jit(solution)/shard_map/ppermute | solution.py:199
  10.0 8.7 %collective-permute-start.2 = (bf16[512,256]{1,0:T(8,128)(2,1)}, bf16[512,256]{1,0:T(8,128)(2,1)S(1)}, u32[]{:S(2)}, u32[]{:S(2)}) collective-permute-start(bf16[512,256]{1,0:T(8,128)(2,1)} %param.5), channel_id=1, source_target_pairs={{0,2},{1,3},{2,4},{3,5},{4,6},{5,7},{6,8},{7,9},{8,10},{9,11},{10,... | collective-permute-start | bytes 786440 | tf_op jit(solution)/shard_map/ppermute | solution.py:199
  13.5 16.3 %collective-permute-start.4 = (bf16[512,256]{1,0:T(8,128)(2,1)}, bf16[512,256]{1,0:T(8,128)(2,1)S(1)}, u32[]{:S(2)}, u32[]{:S(2)}) collective-permute-start(bf16[512,256]{1,0:T(8,128)(2,1)} %param.5), channel_id=1, source_target_pairs={{4,0},{5,1},{6,2},{7,3},{8,4},{9,5},{10,6},{11,7},{12,8},{13,9},{1... | collective-permute-start | bytes 786440 | tf_op jit(solution)/shard_map/ppermute | solution.py:199
  14.8 14.9 %collective-permute-start.3 = (bf16[512,256]{1,0:T(8,128)(2,1)}, bf16[512,256]{1,0:T(8,128)(2,1)S(1)}, u32[]{:S(2)}, u32[]{:S(2)}) collective-permute-start(bf16[512,256]{1,0:T(8,128)(2,1)} %param.5), channel_id=1, source_target_pairs={{2,0},{3,1},{4,2},{5,3},{6,4},{7,5},{8,6},{9,7},{10,8},{11,9},{12,... | collective-permute-start | bytes 786440 | tf_op jit(solution)/shard_map/ppermute | solution.py:199
  16.1 13.7 %collective-permute-start.5 = (bf16[512,256]{1,0:T(8,128)(2,1)}, bf16[512,256]{1,0:T(8,128)(2,1)S(1)}, u32[]{:S(2)}, u32[]{:S(2)}) collective-permute-start(bf16[512,256]{1,0:T(8,128)(2,1)} %param.5), channel_id=1, source_target_pairs={{6,0},{7,1},{8,2},{9,3},{10,4},{11,5},{12,6},{13,7},{14,8},{15,9},... | collective-permute-start | bytes 786440 | tf_op jit(solution)/shard_map/ppermute | solution.py:199
  29.8 3.9 %copy-start = (bf16[3584,256]{1,0:T(8,128)(2,1)}, bf16[3584,256]{1,0:T(8,128)(2,1)S(1)}, u32[]{:S(2)}) copy-start(bf16[3584,256]{1,0:T(8,128)(2,1)S(1)} %constant_dynamic-update-slice_fusion.own_any) | copy-start | bytes 5505028
  29.8 3.9 %collective-permute-start.6 = (bf16[3584,256]{1,0:T(8,128)(2,1)S(1)}, bf16[3584,256]{1,0:T(8,128)(2,1)S(1)}, u32[]{:S(2)}, u32[]{:S(2)}) collective-permute-start(bf16[3584,256]{1,0:T(8,128)(2,1)S(1)} %constant_dynamic-update-slice_fusion.own_any), channel_id=1, source_target_pairs={{0,1},{1,0},{2,3},{3,2},{4,5},{5,4},{6,7},{7,6},{8,9},{9,8},{10,11... | collective-permute-start | bytes 5505032 | tf_op jit(solution)/shard_map/ppermute | solution.py:204
  33.7 1.3 copy-start.1
  52.0 8.5 %collective-permute-start.7 = (bf16[3584,256]{1,0:T(8,128)(2,1)}, bf16[3584,256]{1,0:T(8,128)(2,1)S(1)}, u32[]{:S(2)}, u32[]{:S(2)}) collective-permute-start(bf16[3584,256]{1,0:T(8,128)(2,1)} %get-tuple-element.7), channel_id=1, source_target_pairs={{0,1},{1,0},{2,3},{3,2},{4,5},{5,4},{6,7},{7,6},{8,9},{9,8},{10,11... | collective-permute-start | bytes 5505032 | tf_op jit(solution)/shard_map/ppermute | solution.py:204
  63.2 60.4 %collective-permute-start.8 = (bf16[512,256]{1,0:T(8,128)(2,1)S(1)}, bf16[512,256]{1,0:T(8,128)(2,1)S(1)}, u32[]{:S(2)}, u32[]{:S(2)}) collective-permute-start(bf16[512,256]{1,0:T(8,128)(2,1)S(1)} %get-tuple-element.10), channel_id=1, source_target_pairs={{6,0},{7,1},{8,2},{9,3},{10,4},{11,5},{12,6},{13,7},{14,8},{15,9},... | collective-permute-start | bytes 786440 | tf_op jit(solution)/shard_map/ppermute | solution.py:199
  64.5 60.4 %collective-permute-start.13 = (bf16[512,256]{1,0:T(8,128)(2,1)S(1)}, bf16[512,256]{1,0:T(8,128)(2,1)S(1)}, u32[]{:S(2)}, u32[]{:S(2)}) collective-permute-start(bf16[512,256]{1,0:T(8,128)(2,1)S(1)} %get-tuple-element.11), channel_id=1, source_target_pairs={{0,6},{1,7},{2,8},{3,9},{4,10},{5,11},{6,12},{7,13},{8,14},{9,15},... | collective-permute-start | bytes 786440 | tf_op jit(solution)/shard_map/ppermute | solution.py:199
  111.1 16.0 %collective-permute-start.12 = (bf16[512,256]{1,0:T(8,128)(2,1)S(1)}, bf16[512,256]{1,0:T(8,128)(2,1)S(1)}, u32[]{:S(2)}, u32[]{:S(2)}) collective-permute-start(bf16[512,256]{1,0:T(8,128)(2,1)S(1)} %get-tuple-element.12), channel_id=1, source_target_pairs={{0,4},{1,5},{2,6},{3,7},{4,8},{5,9},{6,10},{7,11},{8,12},{9,13},{1... | collective-permute-start | bytes 786440 | tf_op jit(solution)/shard_map/ppermute | solution.py:199
  116.8 17.9 %collective-permute-start.11 = (bf16[512,256]{1,0:T(8,128)(2,1)S(1)}, bf16[512,256]{1,0:T(8,128)(2,1)S(1)}, u32[]{:S(2)}, u32[]{:S(2)}) collective-permute-start(bf16[512,256]{1,0:T(8,128)(2,1)S(1)} %get-tuple-element.13), channel_id=1, source_target_pairs={{0,2},{1,3},{2,4},{3,5},{4,6},{5,7},{6,8},{7,9},{8,10},{9,11},{10,... | collective-permute-start | bytes 786440 | tf_op jit(solution)/shard_map/ppermute | solution.py:199
  122.2 12.6 %collective-permute-start.10 = (bf16[512,256]{1,0:T(8,128)(2,1)S(1)}, bf16[512,256]{1,0:T(8,128)(2,1)S(1)}, u32[]{:S(2)}, u32[]{:S(2)}) collective-permute-start(bf16[512,256]{1,0:T(8,128)(2,1)S(1)} %get-tuple-element.14), channel_id=1, source_target_pairs={{2,0},{3,1},{4,2},{5,3},{6,4},{7,5},{8,6},{9,7},{10,8},{11,9},{12,... | collective-permute-start | bytes 786440 | tf_op jit(solution)/shard_map/ppermute | solution.py:199
  123.5 14.6 %collective-permute-start.9 = (bf16[512,256]{1,0:T(8,128)(2,1)S(1)}, bf16[512,256]{1,0:T(8,128)(2,1)S(1)}, u32[]{:S(2)}, u32[]{:S(2)}) collective-permute-start(bf16[512,256]{1,0:T(8,128)(2,1)S(1)} %get-tuple-element.15), channel_id=1, source_target_pairs={{4,0},{5,1},{6,2},{7,3},{8,4},{9,5},{10,6},{11,7},{12,8},{13,9},{1... | collective-permute-start | bytes 786440 | tf_op jit(solution)/shard_map/ppermute | solution.py:199

commit v2 on v1

--- a/solution.py
+++ b/solution.py
@@ -12,11 +12,18 @@
 HG = 4
 TILE = 256
 MOST = 12
-STEP = 2
+STEP = 6
 SCALE = HD**-0.5
 SCALE_LOG2 = SCALE * 1.4426950408889634
 F32 = jnp.float32
 BF16 = jnp.bfloat16
+
+
+RELATIONS = ("self", "row", "up", "down", "up_across", "down_across", "two_rows")
+
+
+def chip_step(relation, column):
+    return (0, 1 - 2 * column, 2, -2, 3 - 2 * column, -1 - 2 * column, 6 * column - 3)[relation]
 
 
 def attention_kernel(
@@ -27,10 +34,12 @@
     rows_dev = per_device * TILE
     me = lax.axis_index("dp")
     core = lax.rem(me, 2)
+    column = lax.rem(me // 2, 2)
     base_tile = (me // 2 - reach) * 2 * per_device
 
     def near(piece, which):
-        return pl.ds(pl.multiple_of((piece * 2 + which) * rows_dev, rows_dev), rows_dev)
+        place = reach + chip_step(piece, column)
+        return pl.ds(pl.multiple_of((place * 2 + which) * rows_dev, rows_dev), rows_dev)
 
     def far(piece):
         return pl.ds(piece * rows_dev, rows_dev)
@@ -190,30 +199,41 @@
 
 def body(queries, kv_cache, grad_out, pair_lengths):
     rows_dev = queries.shape[0]
-    per_chip = 2 * rows_dev // TILE
-    reach = (MOST - 1 + per_chip - 1) // per_chip
+    reach = 3
+    assert 2 * rows_dev * reach >= (MOST - 1) * TILE
     count = lax.axis_size("dp")
 
-    def by_chips(value, chips):
-        steps = 2 * chips
-        return lax.ppermute(
-            value, "dp", [(i, i + steps) for i in range(count) if 0 <= i + steps < count]
-        )
+    def send(value, relation, back):
+        pairs = []
+        for source in range(count):
+            row, column, core = source // 4, (source // 2) % 2, source % 2
+            rows, across = {
+                "row": (0, 1),
+                "up": (1, 0),
+                "down": (-1, 0),
+                "up_across": (1, 1),
+                "down_across": (-1, 1),
+                "two_rows": (4 * column - 2, 1),
+            }[relation]
+            if back and relation != "two_rows":
+                rows = -rows
+            if 0 <= row + rows < count // 4:
+                pairs.append((source, (row + rows) * 4 + (column ^ across) * 2 + core))
+        return lax.ppermute(value, "dp", pairs)
 
     def to_twin(value):
         return lax.ppermute(value, "dp", [(i, i ^ 1) for i in range(count)])
 
     own = jnp.concatenate(
-        [kv_cache if chips == 0 else by_chips(kv_cache, -chips) for chips in range(-reach, reach + 1)], axis=0
+        [kv_cache] + [send(kv_cache, relation, True) for relation in RELATIONS[1:]], axis=0
     )
     twin = to_twin(own)
     grad_queries, own_grad, twin_grad = attention(reach, pair_lengths, own, twin, queries, grad_out)
     summed = own_grad + to_twin(twin_grad).astype(F32)
-    grad_kv = summed[reach * rows_dev : (reach + 1) * rows_dev]
-    for chips in range(-reach, reach + 1):
-        if chips != 0:
-            low = (chips + reach) * rows_dev
-            grad_kv = grad_kv + by_chips(summed[low : low + rows_dev].astype(BF16), chips).astype(F32)
+    grad_kv = summed[:rows_dev]
+    for piece, relation in enumerate(RELATIONS[1:], 1):
+        share = summed[piece * rows_dev : (piece + 1) * rows_dev].astype(BF16)
+        grad_kv = grad_kv + send(share, relation, False).astype(F32)
     return grad_queries, grad_kv
 
 

time: 139 us -> 132 us (0.950)
  waiting for transfers between devices: 31.9 us -> 23.7 us
    ppermute x12, starting transfers between devices: 78.3 us -> 47 us  [send(): return lax.ppermute(value, 'dp', pairs)]
    ppermute x2, starting transfers between devices: 4.94 us -> 35.5 us  [to_twin(): return lax.ppermute(value, 'dp', [(i, i ^ 1) for i in range(count)])]
    ppermute x12, waiting for transfers between devices: 24.5 us -> 16.3 us  [send(): return lax.ppermute(value, 'dp', pairs)]
  transfers between devices with their start and end apart: 14 -> 14, of which waited for: 8 -> 5; matrix products, arithmetic and copies ran while one was open for 1% -> 1% of each run, Pallas kernels for 0% -> 0%
where the time goes in v2:
time: 132 us; the launch traced here: 131 us
  starting transfers between devices  82.6 us (63%)
  waiting for transfers between devices  23.7 us (18%)
  Pallas kernels  18 us (14%)
  other arithmetic  3.6 us (3%)
  local copies, waits for them, and re-layouts  2.48 us (2%)
    ppermute x12, starting transfers between devices, send(): return lax.ppermute(value, 'dp', pairs)  47 us
    ppermute x2, starting transfers between devices, to_twin(): return lax.ppermute(value, 'dp', [(i, i ^ 1) for i in range(count)])  35.5 us
    pallas_call x1, Pallas kernels, attention(): pl.pallas_call(functools.partial(attention_kernel, reach, per_device), ou...  18 us
    ppermute x12, waiting for transfers between devices, send(): return lax.ppermute(value, 'dp', pairs)  16.3 us
    ppermute x2, waiting for transfers between devices, to_twin(): return lax.ppermute(value, 'dp', [(i, i ^ 1) for i in range(count)])  7.39 us
  transfers between devices with their start and end apart: 14, of which 5 were waited for; matrix products, arithmetic and copies ran while one was open for 1% of the time, Pallas kernels for 0%

profile of v2, /device:TPU:0, one launch (start us, length us, event | category | flops | bytes accessed | tf_op | source)
XLA Modules:
  0.0 131.2 jit_solution(260992293034050121)
XLA Ops:
  0.6 3.0 %collective-permute-start = (bf16[512,256]{1,0:T(8,128)(2,1)}, bf16[512,256]{1,0:T(8,128)(2,1)S(1)}, u32[]{:S(2)}, u32[]{:S(2)}) collective-permute-start(bf16[512,256]{1,0:T(8,128)(2,1)} %param.5), channel_id=1, source_target_pairs={{0,2},{1,3},{2,0},{3,1},{4,6},{5,7},{6,4},{7,5},{8,10},{9,11},{10,... | collective-permute-start | bytes 786440 | tf_op jit(solution)/shard_map/ppermute | solution.py:222
  3.7 1.3 collective-permute-start.1
  4.9 4.1 %collective-permute-start.4 = (bf16[512,256]{1,0:T(8,128)(2,1)}, bf16[512,256]{1,0:T(8,128)(2,1)S(1)}, u32[]{:S(2)}, u32[]{:S(2)}) collective-permute-start(bf16[512,256]{1,0:T(8,128)(2,1)} %param.5), channel_id=1, source_target_pairs={{0,6},{1,7},{2,4},{3,5},{4,10},{5,11},{6,8},{7,9},{8,14},{9,15},{1... | collective-permute-start | bytes 786440 | tf_op jit(solution)/shard_map/ppermute | solution.py:222
  9.0 1.3 collective-permute-start.3
  10.3 6.0 %collective-permute-start.2 = (bf16[512,256]{1,0:T(8,128)(2,1)}, bf16[512,256]{1,0:T(8,128)(2,1)S(1)}, u32[]{:S(2)}, u32[]{:S(2)}) collective-permute-start(bf16[512,256]{1,0:T(8,128)(2,1)} %param.5), channel_id=1, source_target_pairs={{0,4},{1,5},{2,6},{3,7},{4,8},{5,9},{6,10},{7,11},{8,12},{9,13},{1... | collective-permute-start | bytes 786440 | tf_op jit(solution)/shard_map/ppermute | solution.py:222
  16.3 1.0 constant_dynamic-update-slice_fusion.6
  17.3 0.0 collective-permute-done
  17.3 0.7 collective-permute-start.5
  18.0 0.0 collective-permute-done.1
  18.1 3.0 %collective-permute-done.2 = bf16[512,256]{1,0:T(8,128)(2,1)S(1)} collective-permute-done((bf16[512,256]{1,0:T(8,128)(2,1)}, bf16[512,256]{1,0:T(8,128)(2,1)S(1)}, u32[]{:S(2)}, u32[]{:S(2)}) %collective-permute-start.2) | collective-permute-done | bytes 262176 | tf_op jit(solution)/shard_map/ppermute | solution.py:222
  21.0 0.0 collective-permute-done.3
  21.1 0.0 collective-permute-done.4
  21.1 0.0 collective-permute-done.5
  21.2 0.0 copy-start
  21.2 0.1 collective-permute-start.6
  21.2 3.8 %collective-permute-done.6.twin_any = bf16[3584,256]{1,0:T(8,128)(2,1)S(1)} collective-permute-done((bf16[3584,256]{1,0:T(8,128)(2,1)S(1)}, bf16[3584,256]{1,0:T(8,128)(2,1)S(1)}, u32[]{:S(2)}, u32[]{:S(2)}) %collective-permute-start.6) | collective-permute-done | bytes 1835040 | tf_op jit(solution)/shard_map/ppermute | solution.py:225
  25.0 0.0 copy-done
  25.0 0.0 copy-start.1
  25.0 1.2 copy-done.1
  26.3 18.0 %shard_map.59 = (bf16[512,1024]{1,0:T(8,128)(2,1)}, f32[3584,256]{1,0:T(8,128)}, bf16[3584,256]{1,0:T(8,128)(2,1)}) custom-call(s32[10]{0:T(128)} %lengths.1, bf16[3584,256]{1,0:T(8,128)(2,1)} %copy-done, bf16[3584,256]{1,0:T(8,128)(2,1)} %copy-done.1, bf16[512,1024]{1,0:T(8,128)(2,1)} %q_ref.1, bf16[512,1024]{1,0:T(8,128)(2,1)} %g_ref.1), custom_call_target="tpu_custom_call" | custom-call | tf_op jit(solution)/shard_map/pallas_call | solution.py:173
  44.3 35.5 %collective-permute-start.7 = (bf16[3584,256]{1,0:T(8,128)(2,1)}, bf16[3584,256]{1,0:T(8,128)(2,1)S(1)}, u32[]{:S(2)}, u32[]{:S(2)}) collective-permute-start(bf16[3584,256]{1,0:T(8,128)(2,1)} %get-tuple-element.7), channel_id=1, source_target_pairs={{0,1},{1,0},{2,3},{3,2},{4,5},{5,4},{6,7},{7,6},{8,9},{9,8},{10,11... | collective-permute-start | bytes 5505032 | tf_op jit(solution)/shard_map/ppermute | solution.py:225
  79.7 3.6 %collective-permute-done.7 = bf16[3584,256]{1,0:T(8,128)(2,1)S(1)} collective-permute-done((bf16[3584,256]{1,0:T(8,128)(2,1)}, bf16[3584,256]{1,0:T(8,128)(2,1)S(1)}, u32[]{:S(2)}, u32[]{:S(2)}) %collective-permute-start.7) | collective-permute-done | bytes 1835040 | tf_op jit(solution)/shard_map/ppermute | solution.py:225
  83.4 2.6 %fusion.5 = (bf16[3584,256]{1,0:T(8,128)(2,1)S(1)}, f32[3584,256]{1,0:T(8,128)S(1)}) fusion(f32[3584,256]{1,0:T(8,128)} %get-tuple-element.6, bf16[3584,256]{1,0:T(8,128)(2,1)S(1)} %collective-permute-done.7), kind=kLoop, calls=%fused_computation.14 | loop fusion | flops 2752512 | bytes 11010048 | tf_op jit(solution)/shard_map/convert.5
  85.9 0.1 fusion.6
  86.0 13.9 %collective-permute-start.8 = (bf16[512,256]{1,0:T(8,128)(2,1)S(1)}, bf16[512,256]{1,0:T(8,128)(2,1)S(1)}, u32[]{:S(2)}, u32[]{:S(2)}) collective-permute-start(bf16[512,256]{1,0:T(8,128)(2,1)S(1)} %get-tuple-element.10), channel_id=1, source_target_pairs={{0,2},{1,3},{2,0},{3,1},{4,6},{5,7},{6,4},{7,5},{8,10},{9,11},{10,... | collective-permute-start | bytes 786440 | tf_op jit(solution)/shard_map/ppermute | solution.py:222
  100.0 0.7 collective-permute-start.13
  100.6 1.3 collective-permute-start.12
  101.9 5.5 %collective-permute-start.11 = (bf16[512,256]{1,0:T(8,128)(2,1)S(1)}, bf16[512,256]{1,0:T(8,128)(2,1)S(1)}, u32[]{:S(2)}, u32[]{:S(2)}) collective-permute-start(bf16[512,256]{1,0:T(8,128)(2,1)S(1)} %get-tuple-element.13), channel_id=1, source_target_pairs={{0,6},{1,7},{2,4},{3,5},{4,10},{5,11},{6,8},{7,9},{8,14},{9,15},{1... | collective-permute-start | bytes 786440 | tf_op jit(solution)/shard_map/ppermute | solution.py:222
  107.4 1.3 collective-permute-start.10
  108.7 8.4 %collective-permute-done.8 = bf16[512,256]{1,0:T(8,128)(2,1)S(1)} collective-permute-done((bf16[512,256]{1,0:T(8,128)(2,1)S(1)}, bf16[512,256]{1,0:T(8,128)(2,1)S(1)}, u32[]{:S(2)}, u32[]{:S(2)}) %collective-permute-start.8) | collective-permute-done | bytes 262176 | tf_op jit(solution)/shard_map/ppermute | solution.py:222
  117.1 8.1 %collective-permute-start.9 = (bf16[512,256]{1,0:T(8,128)(2,1)S(1)}, bf16[512,256]{1,0:T(8,128)(2,1)S(1)}, u32[]{:S(2)}, u32[]{:S(2)}) collective-permute-start(bf16[512,256]{1,0:T(8,128)(2,1)S(1)} %get-tuple-element.15), channel_id=1, source_target_pairs={{0,4},{1,5},{2,6},{3,7},{4,8},{5,9},{6,10},{7,11},{8,12},{9,13},{1... | collective-permute-start | bytes 786440 | tf_op jit(solution)/shard_map/ppermute | solution.py:222
  125.2 0.0 collective-permute-done.13
  125.2 0.0 collective-permute-done.12
  125.2 0.0 collective-permute-done.11
  125.2 0.0 collective-permute-done.10
  125.2 5.0 %collective-permute-done.9 = bf16[512,256]{1,0:T(8,128)(2,1)S(1)} collective-permute-done((bf16[512,256]{1,0:T(8,128)(2,1)S(1)}, bf16[512,256]{1,0:T(8,128)(2,1)S(1)}, u32[]{:S(2)}, u32[]{:S(2)}) %collective-permute-start.9) | collective-permute-done | bytes 262176 | tf_op jit(solution)/shard_map/ppermute | solution.py:222
  130.2 1.0 fusion.4
  (6 shorter events, 0.1 us)
Async XLA Ops:
  0.6 16.7 %collective-permute-start = (bf16[512,256]{1,0:T(8,128)(2,1)}, bf16[512,256]{1,0:T(8,128)(2,1)S(1)}, u32[]{:S(2)}, u32[]{:S(2)}) collective-permute-start(bf16[512,256]{1,0:T(8,128)(2,1)} %param.5), channel_id=1, source_target_pairs={{0,2},{1,3},{2,0},{3,1},{4,6},{5,7},{6,4},{7,5},{8,10},{9,11},{10,... | collective-permute-start | bytes 786440 | tf_op jit(solution)/shard_map/ppermute | solution.py:222
  3.7 14.4 %collective-permute-start.1 = (bf16[512,256]{1,0:T(8,128)(2,1)}, bf16[512,256]{1,0:T(8,128)(2,1)S(1)}, u32[]{:S(2)}, u32[]{:S(2)}) collective-permute-start(bf16[512,256]{1,0:T(8,128)(2,1)} %param.5), channel_id=1, source_target_pairs={{4,0},{5,1},{6,2},{7,3},{8,4},{9,5},{10,6},{11,7},{12,8},{13,9},{1... | collective-permute-start | bytes 786440 | tf_op jit(solution)/shard_map/ppermute | solution.py:222
  4.9 16.1 %collective-permute-start.4 = (bf16[512,256]{1,0:T(8,128)(2,1)}, bf16[512,256]{1,0:T(8,128)(2,1)S(1)}, u32[]{:S(2)}, u32[]{:S(2)}) collective-permute-start(bf16[512,256]{1,0:T(8,128)(2,1)} %param.5), channel_id=1, source_target_pairs={{0,6},{1,7},{2,4},{3,5},{4,10},{5,11},{6,8},{7,9},{8,14},{9,15},{1... | collective-permute-start | bytes 786440 | tf_op jit(solution)/shard_map/ppermute | solution.py:222
  9.0 12.0 %collective-permute-start.3 = (bf16[512,256]{1,0:T(8,128)(2,1)}, bf16[512,256]{1,0:T(8,128)(2,1)S(1)}, u32[]{:S(2)}, u32[]{:S(2)}) collective-permute-start(bf16[512,256]{1,0:T(8,128)(2,1)} %param.5), channel_id=1, source_target_pairs={{4,2},{5,3},{6,0},{7,1},{8,6},{9,7},{10,4},{11,5},{12,10},{13,11},... | collective-permute-start | bytes 786440 | tf_op jit(solution)/shard_map/ppermute | solution.py:222
  10.3 10.7 %collective-permute-start.2 = (bf16[512,256]{1,0:T(8,128)(2,1)}, bf16[512,256]{1,0:T(8,128)(2,1)S(1)}, u32[]{:S(2)}, u32[]{:S(2)}) collective-permute-start(bf16[512,256]{1,0:T(8,128)(2,1)} %param.5), channel_id=1, source_target_pairs={{0,4},{1,5},{2,6},{3,7},{4,8},{5,9},{6,10},{7,11},{8,12},{9,13},{1... | collective-permute-start | bytes 786440 | tf_op jit(solution)/shard_map/ppermute | solution.py:222
  17.3 3.8 %collective-permute-start.5 = (bf16[512,256]{1,0:T(8,128)(2,1)}, bf16[512,256]{1,0:T(8,128)(2,1)S(1)}, u32[]{:S(2)}, u32[]{:S(2)}) collective-permute-start(bf16[512,256]{1,0:T(8,128)(2,1)} %param.5), channel_id=1, source_target_pairs={{2,8},{3,9},{6,12},{7,13},{8,2},{9,3},{12,6},{13,7},{18,24},{19,25... | collective-permute-start | bytes 786440 | tf_op jit(solution)/shard_map/ppermute | solution.py:222
  21.2 3.9 %copy-start = (bf16[3584,256]{1,0:T(8,128)(2,1)}, bf16[3584,256]{1,0:T(8,128)(2,1)S(1)}, u32[]{:S(2)}) copy-start(bf16[3584,256]{1,0:T(8,128)(2,1)S(1)} %constant_dynamic-update-slice_fusion.own_any) | copy-start | bytes 5505028
  21.2 3.9 %collective-permute-start.6 = (bf16[3584,256]{1,0:T(8,128)(2,1)S(1)}, bf16[3584,256]{1,0:T(8,128)(2,1)S(1)}, u32[]{:S(2)}, u32[]{:S(2)}) collective-permute-start(bf16[3584,256]{1,0:T(8,128)(2,1)S(1)} %constant_dynamic-update-slice_fusion.own_any), channel_id=1, source_target_pairs={{0,1},{1,0},{2,3},{3,2},{4,5},{5,4},{6,7},{7,6},{8,9},{9,8},{10,11... | collective-permute-start | bytes 5505032 | tf_op jit(solution)/shard_map/ppermute | solution.py:225
  25.0 1.3 copy-start.1
  44.3 39.1 %collective-permute-start.7 = (bf16[3584,256]{1,0:T(8,128)(2,1)}, bf16[3584,256]{1,0:T(8,128)(2,1)S(1)}, u32[]{:S(2)}, u32[]{:S(2)}) collective-permute-start(bf16[3584,256]{1,0:T(8,128)(2,1)} %get-tuple-element.7), channel_id=1, source_target_pairs={{0,1},{1,0},{2,3},{3,2},{4,5},{5,4},{6,7},{7,6},{8,9},{9,8},{10,11... | collective-permute-start | bytes 5505032 | tf_op jit(solution)/shard_map/ppermute | solution.py:225
  86.0 31.0 %collective-permute-start.8 = (bf16[512,256]{1,0:T(8,128)(2,1)S(1)}, bf16[512,256]{1,0:T(8,128)(2,1)S(1)}, u32[]{:S(2)}, u32[]{:S(2)}) collective-permute-start(bf16[512,256]{1,0:T(8,128)(2,1)S(1)} %get-tuple-element.10), channel_id=1, source_target_pairs={{0,2},{1,3},{2,0},{3,1},{4,6},{5,7},{6,4},{7,5},{8,10},{9,11},{10,... | collective-permute-start | bytes 786440 | tf_op jit(solution)/shard_map/ppermute | solution.py:222
  100.0 25.2 %collective-permute-start.13 = (bf16[512,256]{1,0:T(8,128)(2,1)S(1)}, bf16[512,256]{1,0:T(8,128)(2,1)S(1)}, u32[]{:S(2)}, u32[]{:S(2)}) collective-permute-start(bf16[512,256]{1,0:T(8,128)(2,1)S(1)} %get-tuple-element.11), channel_id=1, source_target_pairs={{2,8},{3,9},{6,12},{7,13},{8,2},{9,3},{12,6},{13,7},{18,24},{19,25... | collective-permute-start | bytes 786440 | tf_op jit(solution)/shard_map/ppermute | solution.py:222
  100.6 24.5 %collective-permute-start.12 = (bf16[512,256]{1,0:T(8,128)(2,1)S(1)}, bf16[512,256]{1,0:T(8,128)(2,1)S(1)}, u32[]{:S(2)}, u32[]{:S(2)}) collective-permute-start(bf16[512,256]{1,0:T(8,128)(2,1)S(1)} %get-tuple-element.12), channel_id=1, source_target_pairs={{4,2},{5,3},{6,0},{7,1},{8,6},{9,7},{10,4},{11,5},{12,10},{13,11},... | collective-permute-start | bytes 786440 | tf_op jit(solution)/shard_map/ppermute | solution.py:222
  101.9 23.2 %collective-permute-start.11 = (bf16[512,256]{1,0:T(8,128)(2,1)S(1)}, bf16[512,256]{1,0:T(8,128)(2,1)S(1)}, u32[]{:S(2)}, u32[]{:S(2)}) collective-permute-start(bf16[512,256]{1,0:T(8,128)(2,1)S(1)} %get-tuple-element.13), channel_id=1, source_target_pairs={{0,6},{1,7},{2,4},{3,5},{4,10},{5,11},{6,8},{7,9},{8,14},{9,15},{1... | collective-permute-start | bytes 786440 | tf_op jit(solution)/shard_map/ppermute | solution.py:222
  107.4 17.8 %collective-permute-start.10 = (bf16[512,256]{1,0:T(8,128)(2,1)S(1)}, bf16[512,256]{1,0:T(8,128)(2,1)S(1)}, u32[]{:S(2)}, u32[]{:S(2)}) collective-permute-start(bf16[512,256]{1,0:T(8,128)(2,1)S(1)} %get-tuple-element.14), channel_id=1, source_target_pairs={{4,0},{5,1},{6,2},{7,3},{8,4},{9,5},{10,6},{11,7},{12,8},{13,9},{1... | collective-permute-start | bytes 786440 | tf_op jit(solution)/shard_map/ppermute | solution.py:222
  117.1 13.1 %collective-permute-start.9 = (bf16[512,256]{1,0:T(8,128)(2,1)S(1)}, bf16[512,256]{1,0:T(8,128)(2,1)S(1)}, u32[]{:S(2)}, u32[]{:S(2)}) collective-permute-start(bf16[512,256]{1,0:T(8,128)(2,1)S(1)} %get-tuple-element.15), channel_id=1, source_target_pairs={{0,4},{1,5},{2,6},{3,7},{4,8},{5,9},{6,10},{7,11},{8,12},{9,13},{1... | collective-permute-start | bytes 786440 | tf_op jit(solution)/shard_map/ppermute | solution.py:222
